TPU v7x, 32 devices: a whole 2x2x4 slice. The times are simulated.
32 devices in a mesh: expert: 8 (over y, x, core), tensor: 4 (over z).
Axes of the slice: x: 2, y: 2, z: 4, core: 2. Of those that a mesh axis runs over, the one named last changes fastest.
Arguments:
- picked_rows: bfloat16 [8, 256, 6144], P('expert', None, 'tensor'), may hold values from -6 to 6
- w_gate: bfloat16 [8, 6144, 1536], P('expert', 'tensor'), may hold values from -0.078125 to 0.078125
- w_up: bfloat16 [8, 6144, 1536], P('expert', 'tensor'), may hold values from -0.078125 to 0.078125
- w_down: bfloat16 [8, 1536, 6144], P('expert', None, 'tensor'), may hold values from -0.15625 to 0.15625
- combine_gate: float32 [8, 256], P('expert'), may hold values from 0.3 to 3
- pick_owner: int32 [8, 256], replicated, may hold values from 0 to 7, as said below
- pick_row: int32 [8, 256], replicated, may hold values from 0 to 191, as said below
- residual_in: bfloat16 [1536, 6144], P('expert', 'tensor'), may hold values from -60 to 60
- norm_gain: float32 [6144], P('tensor'), may hold values from 0.5 to 2
- projection: bfloat16 [6144, 6144], P('expert', 'tensor'), may hold values from -0.078125 to 0.078125
Outputs:
- projected: bfloat16 [1536, 6144], P('expert', 'tensor')
Inputs may be any that keep to these rules, and one draw needn't show every extreme that they name: `pick_owner`: for every expert, at most 96 of its picks have one owner group, and one owner group gets exactly 96 picks from every expert. The picks of one expert are distinct tokens. `pick_row`: together with pick_owner it names a token; no expert names a token twice.
All inputs are finite; a program needn't handle non-finite values.
Results may differ from a plain program's by a relative error of at most 0.0051.
Values may be sent and summed in bfloat16 or wider, within the bound.
A program may use at most 64 MiB of HBM per device.

v0:
```python
import jax
import jax.numpy as jnp
from jax import lax
from jax.sharding import PartitionSpec as P

D = 6144


def shards(
    picked_rows,
    w_gate,
    w_up,
    w_down,
    combine_gate,
    pick_owner,
    pick_row,
    residual_in,
    norm_gain,
    projection,
):
    my_rows = picked_rows[0]
    gate_mat = w_gate[0]
    up_mat = w_up[0]
    down_mat = w_down[0]
    capacity = my_rows.shape[0]
    gate_part = jnp.dot(my_rows, gate_mat, preferred_element_type=jnp.float32)
    up_part = jnp.dot(my_rows, up_mat, preferred_element_type=jnp.float32)
    gate_pre, up_pre = lax.psum((gate_part, up_part), "tensor")
    hidden = (jax.nn.silu(gate_pre) * up_pre).astype(jnp.bfloat16)
    expert_out = jnp.dot(hidden, down_mat, preferred_element_type=jnp.float32)
    weighted = (combine_gate[0][:, None] * expert_out).astype(jnp.bfloat16)
    n_groups = pick_owner.shape[0]
    slot_most = max(3 * capacity // n_groups, 2)
    my_index = lax.axis_index("expert")
    group_ids = jnp.arange(n_groups, dtype=jnp.int32)
    owner_hits = (pick_owner[:, :, None] == group_ids[None, None, :]).astype(jnp.int32)
    earlier = jnp.cumsum(owner_hits, axis=1) - owner_hits
    position = jnp.sum(earlier * owner_hits, axis=2)
    my_owner = lax.dynamic_index_in_dim(pick_owner, my_index, 0, keepdims=False)
    my_position = lax.dynamic_index_in_dim(position, my_index, 0, keepdims=False)
    my_slot = my_owner * slot_most + my_position
    slot_ids = jnp.arange(n_groups * slot_most, dtype=jnp.int32)
    send_table = (my_slot[None, :] == slot_ids[:, None]).astype(jnp.bfloat16)
    outgoing = jnp.dot(send_table, weighted, preferred_element_type=jnp.float32).astype(
        jnp.bfloat16
    )
    outgoing = outgoing.reshape(n_groups, slot_most, weighted.shape[1])
    received = lax.all_to_all(outgoing, "expert", split_axis=0, concat_axis=0, tiled=True)
    mine = pick_owner == my_index
    slot_range = jnp.arange(slot_most, dtype=jnp.int32)
    matches = mine[:, None, :] & (position[:, None, :] == slot_range[None, :, None])
    row_of = jnp.sum(jnp.where(matches, pick_row[:, None, :] + 1, 0), axis=2) - 1
    tok_group = residual_in.shape[0]
    token_ids = jnp.arange(tok_group, dtype=jnp.int32)
    recv_table = (row_of.reshape(-1)[None, :] == token_ids[:, None]).astype(jnp.bfloat16)
    moe = jnp.dot(
        recv_table,
        received.reshape(n_groups * slot_most, weighted.shape[1]),
        preferred_element_type=jnp.float32,
    )
    mixed = residual_in.astype(jnp.float32) + moe
    square_total = lax.psum(jnp.sum(mixed * mixed, axis=1), "tensor")
    inverse_rms = lax.rsqrt(square_total / D + 1e-05)
    normed = (mixed * inverse_rms[:, None] * norm_gain[None, :]).astype(jnp.bfloat16)
    full_normed = lax.all_gather(normed, "tensor", axis=1, tiled=True)
    projected = jnp.dot(
        full_normed,
        lax.all_gather(projection, "expert", axis=0, tiled=True),
        preferred_element_type=jnp.float32,
    )
    return projected.astype(jnp.bfloat16)


def solution(mesh):
    return jax.shard_map(
        shards,
        mesh=mesh,
        in_specs=(
            P("expert", None, "tensor"),
            P("expert", "tensor", None),
            P("expert", "tensor", None),
            P("expert", None, "tensor"),
            P("expert", None),
            P(),
            P(),
            P("expert", "tensor"),
            P("tensor"),
            P("expert", "tensor"),
        ),
        out_specs=P("expert", "tensor"),
        check_vma=False,
    )
```

profile of v0, /device:TPU:0, one launch (start us, length us, event | category | flops | bytes accessed | tf_op | source)
XLA Modules:
  0.0 359.1 jit_solution(12677700122482646932)
XLA Ops:
  6.5 1.1 copy-done
  7.7 5.0 %fusion.2 = f32[256,1536]{1,0:T(8,128)} fusion(bf16[1,1536,1536]{2,1,0:T(8,128)(2,1)} %param.12, bf16[1,256,1536]{2,1,0:T(8,128)(2,1)S(1)} %copy-done), kind=kOutput, calls=%fused_computation.2 | convolution fusion | flops 1207959552 | bytes 7077888 | tf_op jit(solution)/shard_map/dot_general | solution.py:27
  12.7 2.6 fusion.4
  15.3 0.7 copy-done.1
  16.0 4.5 %reduce-window.6 = s32[8,8,2,128]{3,1,2,0:T(8,128)S(1)} reduce-window(s32[8,8,2,128]{3,1,2,0:T(8,128)S(1)} %fusion.24, s32[]{:T(128)} %constant.27.clone.1), window={size=1x1x1x128 pad=0_0x0_0x0_0x127_0}, to_apply=%region_0.0 | reduce-window | flops 2080768 | bytes 131076 | tf_op jit(solution)/shard_map/reduce-window
  20.5 0.1 slice.8
  20.6 0.2 copy.18
  20.8 0.1 fusion.25
  20.9 0.1 fusion.23
  21.0 118.6 %all-reduce.3.cloned.1.call-done = (f32[256,1536]{1,0:T(8,128)}, f32[256,1536]{1,0:T(8,128)}) async-done(((f32[256,1536]{1,0:T(8,128)}, f32[256,1536]{1,0:T(8,128)}), (f32[256,1536]{1,0:T(8,128)}, f32[256,1536]{1,0:T(8,128)})) %all-reduce.3.cloned.1.call-update) | async-done | bytes 3145744 | tf_op jit(solution)/shard_map/psum | solution.py:28
  139.6 6.7 %convolution_convert_fusion = bf16[768,1536]{1,0:T(8,128)(2,1)} fusion(bf16[1,1536,1536]{2,1,0:T(8,128)(2,1)} %param.13, f32[256,1536]{1,0:T(8,128)} %get-tuple-element.5, f32[256,1536]{1,0:T(8,128)} %get-tuple-element.6, f32[256]{0:T(256)S(1)} %bitcast.43, s32[256]{0:T(256)S(1)} %bitcast.42), kind=kOutput, calls=%fused_computation.6 | convolution fusion | flops 1816461312 | bytes 10225664 | tf_op jit(solution)/shard_map/dot_general | solution.py:44
  146.3 3.8 %all-to-all-start = ((bf16[8,96,1536]{2,1,0:T(8,128)(2,1)}), bf16[8,96,1536]{2,1,0:T(8,128)(2,1)S(1)}, u32[]{:S(2)}, u32[]{:S(2)}) async-start(bf16[8,96,1536]{2,1,0:T(8,128)(2,1)} %bitcast.40), calls=%async_computation | async-start | bytes 4718592 | tf_op jit(solution)/shard_map/all_to_all | solution.py:48
  150.1 0.0 all-gather.3.cloned.1.call-start
  150.2 0.2 select_reduce_fusion
  150.5 0.1 sub.11
  150.6 29.0 %all-to-all-done = bf16[8,96,1536]{2,1,0:T(8,128)(2,1)S(1)} async-done(((bf16[8,96,1536]{2,1,0:T(8,128)(2,1)}), bf16[8,96,1536]{2,1,0:T(8,128)(2,1)S(1)}, u32[]{:S(2)}, u32[]{:S(2)}) %all-to-all-start) | async-done | bytes 2359328 | tf_op jit(solution)/shard_map/all_to_all | solution.py:48
  179.6 2.7 multiply_reduce_fusion
  182.3 9.6 %psum.23 = f32[192]{0:T(256)S(1)} all-reduce(f32[192]{0:T(256)S(1)} %get-tuple-element.7), channel_id=1, replica_groups=mesh['expert'=8,'tensor'=4] {'tensor'}, use_global_device_ids=true, to_apply=%region_7.8 | all-reduce | flops 192 | bytes 1536 | tf_op jit(solution)/shard_map/psum | solution.py:62
  192.0 2.3 multiply_convert_fusion.1
  194.3 0.0 all-gather.5.cloned.1.call-start
  194.3 0.7 all-gather.5.cloned.1.call-update
  195.0 46.4 %all-gather.3.cloned.1.call-done = bf16[192,6144]{1,0:T(8,128)(2,1)} async-done(((bf16[192,1536]{1,0:T(8,128)(2,1)}), bf16[192,6144]{1,0:T(8,128)(2,1)}) %all-gather.3.cloned.1.call-update) | async-done | bytes 2359312 | tf_op jit(solution)/shard_map/all_gather | solution.py:65
  241.4 99.5 %all-gather.5.cloned.1.call-done = bf16[6144,1536]{1,0:T(8,128)(2,1)} async-done(((bf16[768,1536]{1,0:T(8,128)(2,1)}), bf16[6144,1536]{1,0:T(8,128)(2,1)}) %all-gather.5.cloned.1.call-update) | async-done | bytes 18874384 | tf_op jit(solution)/shard_map/all_gather | solution.py:68
  340.9 11.7 %convolution_convert_fusion.1 = bf16[192,1536]{1,0:T(8,128)(2,1)} fusion(bf16[192,6144]{1,0:T(8,128)(2,1)} %all-gather.3.cloned.1.call-done, bf16[6144,1536]{1,0:T(8,128)(2,1)} %all-gather.5.cloned.1.call-done), kind=kOutput, calls=%fused_computation.10 | convolution fusion | flops 3624173568 | bytes 21823488 | tf_op jit(solution)/shard_map/dot_general | solution.py:66
  (22 shorter events, 0.1 us)
Async XLA Ops:
  6.5 1.1 copy-start
  6.5 133.1 %all-reduce.3.cloned.1.call-start = ((), (), s32[]{:S(2)}) async-start(), calls=%async_computation.3 | async-start | bytes 6291456 | tf_op jit(solution)/shard_map/psum | solution.py:28
  7.7 5.0 %copy-start.4 = (bf16[1,1536,1536]{2,1,0:T(8,128)(2,1)S(1)}, bf16[1,1536,1536]{2,1,0:T(8,128)(2,1)}, u32[]{:S(2)}) copy-start(bf16[1,1536,1536]{2,1,0:T(8,128)(2,1)} %param.11) | copy-start | bytes 14155780
  15.3 0.7 copy-start.1
  15.3 124.3 %copy-start.5 = (f32[1,256]{1,0:T(1,128)S(1)}, f32[1,256]{1,0:T(1,128)}, u32[]{:S(2)}) copy-start(f32[1,256]{1,0:T(1,128)} %param.14) | copy-start | bytes 3076
  146.3 3.9 %copy-start.3 = (s32[8,256]{1,0:T(8,128)S(1)}, s32[8,256]{1,0:T(8,128)}, u32[]{:S(2)}) copy-start(s32[8,256]{1,0:T(8,128)} %param.16) | copy-start | bytes 24580
  146.3 33.2 %all-to-all-start = ((bf16[8,96,1536]{2,1,0:T(8,128)(2,1)}), bf16[8,96,1536]{2,1,0:T(8,128)(2,1)S(1)}, u32[]{:S(2)}, u32[]{:S(2)}) async-start(bf16[8,96,1536]{2,1,0:T(8,128)(2,1)} %bitcast.40), calls=%async_computation | async-start | bytes 4718592 | tf_op jit(solution)/shard_map/all_to_all | solution.py:48
  150.1 91.2 %all-gather.3.cloned.1.call-start = ((), (), s32[]{:S(2)}) async-start(), calls=%async_computation.1 | async-start | bytes 2949120 | tf_op jit(solution)/shard_map/all_gather | solution.py:65
  179.6 12.4 %copy-start.2 = (f32[1536]{0:T(1024)S(1)}, f32[1536]{0:T(1024)}, u32[]{:S(2)}) copy-start(f32[1536]{0:T(1024)} %param.18) | copy-start | bytes 18436
  194.3 146.6 %all-gather.5.cloned.1.call-start = ((), (), s32[]{:S(2)}) async-start(), calls=%async_computation.2 | async-start | bytes 21233664 | tf_op jit(solution)/shard_map/all_gather | solution.py:68
Sparse Core Ops, SparseCore 0:
  15.4 124.1 all-reduce.2
  194.4 46.9 all-gather.2
  243.3 97.5 all-gather.4
where the time goes:
time: 360 us; the launch traced here: 359 us
  waiting for transfers between devices  294 us (82%)
  matrix products  28.8 us (8%)
  between operations  13.2 us (4%)
  blocking collectives  9.64 us (3%)
  other arithmetic  7.22 us (2%)
  starting transfers between devices  3.87 us (1%)
    psum x1, waiting for transfers between devices, shards(): gate_pre, up_pre = lax.psum((gate_part, up_part), 'tensor')  119 us
    all_gather x1, waiting for transfers between devices, shards(): lax.all_gather(projection, 'expert', axis=0, tiled=True)  99.5 us
    all_gather x1, waiting for transfers between devices, shards(): full_normed = lax.all_gather(normed, 'tensor', axis=1, tiled=True)  46.4 us
    all_to_all x1, waiting for transfers between devices, shards(): lax.all_to_all(outgoing, 'expert', split_axis=0, concat_axis=0, tiled=True)  29 us
    dot_general x1, matrix products, shards(): jnp.dot(full_normed, lax.all_gather(projection, 'expert', axis=0, tiled=T...  11.7 us
    psum x1, blocking collectives, shards(): square_total = lax.psum(jnp.sum(mixed * mixed, axis=1), 'tensor')  9.64 us
  transfers between devices with their start and end apart: 4, of which 4 were waited for; matrix products, arithmetic and copies ran while one was open for 1% of the time, Pallas kernels for 0%

commit v1 on v0

v1 whole, which is shorter than its diff:
```python
import functools
import math

import jax
import jax.numpy as jnp
from jax import lax
from jax.experimental import pallas as pl
from jax.experimental.pallas import tpu as pltpu
from jax.sharding import PartitionSpec as P

MESH = pl.DeviceIdType.MESH
F32 = jnp.float32
BF16 = jnp.bfloat16
HI = lax.Precision.HIGHEST
HALVES = 2


def body(
    n, n_tensor, grid_a, grid_b, width,
    rows_hbm, gate_hbm, up_hbm, down_hbm, combine_ref, owner_ref, row_ref, resid_hbm, gain_ref, proj_hbm,
    out_ref,
    x, wg, wu, wd, resid, part, from_left, from_right, hid, cbuf, ebuf, proj, table, squares, acc,
    load_sem, rs_send, rs_recv, hid_send, hid_recv, c_send, c_recv, c_sib_send, c_sib_recv,
    e_send, e_recv, s_send, s_recv, p_send, p_recv, p_sib_send, p_sib_recv,
):
    e = lax.axis_index("expert")
    z = lax.axis_index("tensor")
    core = lax.rem(e, 2)
    chip = e // 2
    a, b = chip // grid_b, lax.rem(chip, grid_b)
    last = n_tensor - 1
    cap, d_z = x.shape
    ff = wg.shape[1]
    ff_half = ff // HALVES
    seg = cap // n_tensor
    chunks = d_z // width
    tokens = resid.shape[0]
    k_dev = proj_hbm.shape[0]
    k_half = k_dev // 2
    offsets = [(da, db) for da in range(grid_a) for db in range(grid_b)]

    def chip_at(da, db):
        return lax.rem(a + da + grid_a, grid_a) * grid_b + lax.rem(b + db + grid_b, grid_b)

    def to_expert(da, db):
        return {"expert": chip_at(da, db) * 2 + core}

    sibling = {"expert": chip * 2 + 1 - core}

    def remote(src, dst, send, recv, where):
        return pltpu.make_async_remote_copy(
            src_ref=src, dst_ref=dst, send_sem=send, recv_sem=recv, device_id=where, device_id_type=MESH
        )

    loads = [pltpu.make_async_copy(rows_hbm.at[0], x, load_sem.at[0])]
    for h in range(HALVES):
        cols = pl.ds(h * ff_half, ff_half)
        loads.append(pltpu.make_async_copy(gate_hbm.at[0, :, cols], wg.at[:, cols], load_sem.at[1 + 2 * h]))
        loads.append(pltpu.make_async_copy(up_hbm.at[0, :, cols], wu.at[:, cols], load_sem.at[2 + 2 * h]))
    base = 1 + 2 * HALVES
    loads.append(pltpu.make_async_copy(down_hbm.at[0], wd, load_sem.at[base]))
    loads.append(pltpu.make_async_copy(resid_hbm, resid, load_sem.at[base + 1]))
    my_k = pl.multiple_of(e * k_dev, 16)
    loads.append(pltpu.make_async_copy(proj_hbm, proj.at[pl.ds(my_k, k_dev)], load_sem.at[base + 2]))
    for load in loads:
        load.start()

    barrier = pltpu.get_barrier_semaphore()
    for i in range(1, n_tensor):
        pl.semaphore_signal(barrier, inc=1, device_id={"tensor": lax.rem(z + i, n_tensor)}, device_id_type=MESH)
    for da in range(1, grid_a):
        pl.semaphore_signal(barrier, inc=1, device_id=to_expert(da, 0), device_id_type=MESH)
    for db in range(1, grid_b):
        pl.semaphore_signal(barrier, inc=1, device_id=to_expert(0, db), device_id_type=MESH)
    pl.semaphore_signal(barrier, inc=1, device_id=sibling, device_id_type=MESH)
    pl.semaphore_wait(barrier, n_tensor - 1 + grid_a - 1 + grid_b - 1 + 1)

    sends = []

    def begin(copy):
        copy.start()
        sends.append(copy)

    def slot(da, db):
        return da * grid_b + db

    def proj_rows(da, db, k, half=None):
        start = (chip_at(-da, -db) * 2 + k) * k_dev
        if half is None:
            return proj.at[pl.ds(pl.multiple_of(start, 16), k_dev)]
        return proj.at[pl.ds(pl.multiple_of(start + half * k_half, 16), k_half)]

    mine = proj.at[pl.ds(my_k, k_dev)]
    for da, db in offsets[1:]:
        if da == 0 or db == 0:
            begin(remote(proj_hbm, mine, p_send.at[slot(da, db), 0], p_recv.at[slot(da, db), 0], to_expert(da, db)))
    begin(remote(proj_hbm, mine, p_sib_send.at[0], p_sib_recv.at[0], sibling))

    loads[0].wait()
    tile = 256
    for h in range(HALVES):
        loads[1 + 2 * h].wait()
        loads[2 + 2 * h].wait()

        @pl.loop(0, ff_half // tile)
        def _(j):
            src = pl.ds(pl.multiple_of(h * ff_half + j * tile, tile), tile)
            part[h, :, pl.ds(pl.multiple_of(j * tile, tile), tile)] = jnp.dot(
                x[...], wg[:, src], preferred_element_type=F32
            )
            part[h, :, pl.ds(pl.multiple_of(ff_half + j * tile, tile), tile)] = jnp.dot(
                x[...], wu[:, src], preferred_element_type=F32
            )

        @pl.when((z == 0) | (z == last))
        def _():
            for step in range(n_tensor - 1):
                rs_step(step, h, z, last, seg, part, from_left, from_right, rs_send, rs_recv, remote)

    def rs_middle(h):
        @pl.when((z > 0) & (z < last))
        def _():
            for step in range(n_tensor - 1):
                rs_step(step, h, z, last, seg, part, from_left, from_right, rs_send, rs_recv, remote)

    token = lax.broadcasted_iota(jnp.int32, (tokens, cap), 0)
    for da, db in offsets:
        for r in range(2):
            source = chip_at(-da, -db) * 2 + (core if r == 0 else 1 - core)
            owner = owner_ref[pl.ds(source, 1), :]
            row = row_ref[pl.ds(source, 1), :]
            target = jnp.where(owner == e, row, -1)
            table[slot(da, db), r] = jnp.where(target == token, 1.0, 0.0).astype(BF16)

    my_seg = pl.ds(pl.multiple_of(z * seg, seg), seg)
    def rs_final(h):
        @pl.when(z > 0)
        def _():
            remote(from_left.at[h, z], from_left.at[h, z], rs_send.at[0, h, z], rs_recv.at[0, h, z], {"tensor": z}).wait_recv()
            part[h, my_seg, :] += from_left[h, z].astype(F32)

        @pl.when(z < last)
        def _():
            remote(from_right.at[h, z], from_right.at[h, z], rs_send.at[1, h, z], rs_recv.at[1, h, z], {"tensor": z}).wait_recv()
            part[h, my_seg, :] += from_right[h, z].astype(F32)

        gate = part[h, my_seg, :ff_half]
        up = part[h, my_seg, ff_half:]
        hid[h, z] = (gate / (1.0 + jnp.exp(-gate)) * up).astype(BF16)
        chain_own(hid.at[h], hid_send.at[h], hid_recv.at[h], z, last, remote)

    for step in range(n_tensor + HALVES - 1):
        if step < HALVES:
            rs_middle(step)
        for h in range(HALVES):
            if 1 <= step - h < n_tensor:
                chain_pass(step - h, hid.at[h], hid_send.at[h], hid_recv.at[h], z, last, remote)
        if step < HALVES:
            rs_final(step)

    loads[base].wait()
    loads[base + 1].wait()
    weight = lax.dot_general(
        jnp.broadcast_to(combine_ref[...], (8, cap)), jnp.full((8, width), 0.125, F32),
        (((0,), (0,)), ((), ())), precision=HI, preferred_element_type=F32,
    )
    cap_half = cap // 2

    def c_block(q, da, db, r=0, half=None):
        ref = cbuf.at[q, slot(da, db), r]
        return ref if half is None else ref.at[pl.ds(half * cap_half, cap_half)]

    def stage_send(q):
        cols = pl.ds(q * width, width)
        total = 0.0
        for h in range(HALVES):
            total += jnp.dot(
                hid[h].reshape(cap, ff_half), wd[pl.ds(h * ff_half, ff_half), cols], preferred_element_type=F32
            )
        cbuf[q, 0, 0] = (weight * total).astype(BF16)
        own = c_block(q, 0, 0)
        for da, db in offsets[1:]:
            if da == 0 or db == 0:
                s = slot(da, db)
                begin(remote(own, c_block(q, da, db), c_send.at[q, s, 0, 0], c_recv.at[q, s, 0], to_expert(da, db)))
        begin(remote(own, c_block(q, 0, 0, 1), c_sib_send.at[q, 0], c_sib_recv.at[q, 0], sibling))

    def arrived(ref, send, recv):
        remote(ref, ref, send, recv, sibling).wait_recv()

    def stage_forward(q):
        for da, db in offsets[1:]:
            if da != 0 and db != 0:
                continue
            s = slot(da, db)
            block = c_block(q, da, db)
            arrived(block, c_send.at[q, s, 0, 0], c_recv.at[q, s, 0])
            if db == 0:
                for d in range(1, grid_b):
                    t = slot(da, d)
                    begin(remote(c_block(q, da, 0, 0, 0), c_block(q, da, d, 0, 0), c_send.at[q, t, 0, 0], c_recv.at[q, t, 0], to_expert(0, d)))
            else:
                for d in range(1, grid_a):
                    t = slot(d, db)
                    begin(remote(c_block(q, 0, db, 0, 1), c_block(q, d, db, 0, 1), c_send.at[q, t, 1, 0], c_recv.at[q, t, 1], to_expert(d, 0)))
            begin(remote(block, c_block(q, da, db, 1), c_sib_send.at[q, s], c_sib_recv.at[q, s], sibling))

    def stage_combine(q):
        for da, db in offsets:
            if da == 0 or db == 0:
                continue
            s = slot(da, db)
            for half in range(2):
                arrived(c_block(q, da, db, 0, half), c_send.at[q, s, half, 0], c_recv.at[q, s, half])
            block = c_block(q, da, db)
            begin(remote(block, c_block(q, da, db, 1), c_sib_send.at[q, s], c_sib_recv.at[q, s], sibling))
        cols = pl.ds(q * width, width)
        mixed = resid[:, cols].astype(F32)
        for da, db in offsets:
            s = slot(da, db)
            mixed += jnp.dot(table[s, 0], cbuf[q, s, 0], preferred_element_type=F32)
        for da, db in offsets:
            s = slot(da, db)
            arrived(c_block(q, da, db, 1), c_sib_send.at[q, s], c_sib_recv.at[q, s])
            mixed += jnp.dot(table[s, 1], cbuf[q, s, 1], preferred_element_type=F32)
        ebuf[q, z] = (mixed * gain_ref[:, cols]).astype(BF16)
        chain_own(ebuf.at[q], e_send.at[q], e_recv.at[q], z, last, remote)
        return lax.dot_general(
            jnp.ones((8, width), F32), mixed * mixed, (((1,), (1,)), ((), ())), precision=HI,
            preferred_element_type=F32,
        )

    square_sum = 0.0
    for t in range(chunks + 2):
        if t < chunks:
            stage_send(t)
        if 0 <= t - 1 < chunks:
            stage_forward(t - 1)
        if 0 <= t - 2 < chunks:
            square_sum += stage_combine(t - 2)
            for i in range(1, n_tensor):
                if t - 2 - i >= 0:
                    chain_pass(i, ebuf.at[t - 2 - i], e_send.at[t - 2 - i], e_recv.at[t - 2 - i], z, last, remote)
        if t == chunks:
            for da, db in offsets[1:]:
                if da != 0 and db != 0:
                    continue
                s = slot(da, db)
                block = proj_rows(da, db, core)
                arrived(block, p_send.at[s, 0], p_recv.at[s, 0])
                if db == 0:
                    for d in range(1, grid_b):
                        u = slot(da, d)
                        ref = proj_rows(da, 0, core, 0)
                        begin(remote(ref, ref, p_send.at[u, 0], p_recv.at[u, 0], to_expert(0, d)))
                else:
                    for d in range(1, grid_a):
                        u = slot(d, db)
                        ref = proj_rows(0, db, core, 1)
                        begin(remote(ref, ref, p_send.at[u, 1], p_recv.at[u, 1], to_expert(d, 0)))
                begin(remote(block, block, p_sib_send.at[s], p_sib_recv.at[s], sibling))

    squares[z] = square_sum
    for i in range(1, n_tensor):
        begin(remote(squares.at[z], squares.at[z], s_send.at[i], s_recv.at[i], {"tensor": lax.rem(z + i, n_tensor)}))
    for step in range(chunks - n_tensor, chunks + n_tensor):
        for i in range(1, n_tensor):
            q = step - i
            if 0 <= q < chunks and q + i > chunks - 1:
                chain_pass(i, ebuf.at[q], e_send.at[q], e_recv.at[q], z, last, remote)

    total_squares = squares[z]
    for i in range(1, n_tensor):
        origin = lax.rem(z + n_tensor - i, n_tensor)
        remote(squares.at[origin], squares.at[origin], s_send.at[i], s_recv.at[i], {"tensor": z}).wait_recv()
        total_squares += squares[origin]
    col = 512 if d_z % 512 == 0 else 128
    column_total = lax.dot_general(
        total_squares, jnp.full((8, col), 0.125, F32), (((0,), (0,)), ((), ())), precision=HI,
        preferred_element_type=F32,
    )
    inverse_rms = lax.rsqrt(column_total / (d_z * n_tensor) + 1e-05)

    loads[base + 2].wait()
    order = [o for o in offsets if o[0] == 0 or o[1] == 0] + [o for o in offsets if o[0] != 0 and o[1] != 0]
    for da, db in order:
        if da != 0 and db != 0:
            s = slot(da, db)
            for half in range(2):
                arrived(proj_rows(da, db, core, half), p_send.at[s, half], p_recv.at[s, half])
            block = proj_rows(da, db, core)
            begin(remote(block, block, p_sib_send.at[s], p_sib_recv.at[s], sibling))
    for pos, (da, db) in enumerate(order):
        s = slot(da, db)
        arrived(proj_rows(da, db, 1 - core), p_sib_send.at[s], p_sib_recv.at[s])
        source = chip_at(-da, -db)

        @pl.loop(0, d_z // col)
        def _(j):
            cols = pl.ds(pl.multiple_of(j * col, col), col)
            total = 0.0 if pos == 0 else acc[:, cols]
            for q in range(chunks):
                k = pl.ds(pl.multiple_of(source * 2 * k_dev + q * width, 128), width)
                total += jnp.dot(ebuf[q, source], proj[k, cols], preferred_element_type=F32)
            if pos == len(order) - 1:
                out_ref[:, cols] = (total * inverse_rms).astype(BF16)
            else:
                acc[:, cols] = total

    for copy in sends:
        copy.wait_send()
    for h in range(HALVES):
        for step in range(n_tensor - 1):
            right, left = n_tensor - 1 - step, step

            @pl.when(z < right)
            def _():
                remote(from_left.at[h, right], from_left.at[h, right], rs_send.at[0, h, right], rs_recv.at[0, h, right], {"tensor": z + 1}).wait_send()

            @pl.when(z > left)
            def _():
                remote(from_right.at[h, left], from_right.at[h, left], rs_send.at[1, h, left], rs_recv.at[1, h, left], {"tensor": z - 1}).wait_send()
        chain_end(hid.at[h], hid_send.at[h], hid_recv.at[h], z, last, remote)
    for q in range(chunks):
        chain_end(ebuf.at[q], e_send.at[q], e_recv.at[q], z, last, remote)


def rs_step(step, h, z, last, seg, part, from_left, from_right, send, recv, remote):
    right, left = last - step, step

    def go_right():
        @pl.when(z < right)
        def _():
            block = part[h, pl.ds(right * seg, seg), :]
            slot = from_left.at[h, right]
            copy = remote(slot, slot, send.at[0, h, right], recv.at[0, h, right], {"tensor": z + 1})

            @pl.when(z > 0)
            def _():
                copy.wait_recv()
                from_left[h, right] = (from_left[h, right].astype(F32) + block).astype(BF16)

            @pl.when(z == 0)
            def _():
                from_left[h, right] = block.astype(BF16)

            copy.start()

    def go_left():
        @pl.when(z > left)
        def _():
            block = part[h, pl.ds(left * seg, seg), :]
            slot = from_right.at[h, left]
            copy = remote(slot, slot, send.at[1, h, left], recv.at[1, h, left], {"tensor": z - 1})

            @pl.when(z < last)
            def _():
                copy.wait_recv()
                from_right[h, left] = (from_right[h, left].astype(F32) + block).astype(BF16)

            @pl.when(z == last)
            def _():
                from_right[h, left] = block.astype(BF16)

            copy.start()

    @pl.when(2 * z < last)
    def _():
        go_right()
        go_left()

    @pl.when(2 * z >= last)
    def _():
        go_left()
        go_right()


def chain_copy(buf, send, recv, origin, way, target, remote):
    return remote(buf.at[origin], buf.at[origin], send.at[way, origin], recv.at[way, origin], {"tensor": target})


def chain_own(buf, send, recv, z, last, remote):
    @pl.when(z < last)
    def _():
        chain_copy(buf, send, recv, z, 0, z + 1, remote).start()

    @pl.when(z > 0)
    def _():
        chain_copy(buf, send, recv, z, 1, z - 1, remote).start()


def chain_pass(i, buf, send, recv, z, last, remote):
    @pl.when(z >= i)
    def _():
        copy = chain_copy(buf, send, recv, z - i, 0, z + 1, remote)
        copy.wait_recv()

        @pl.when(z < last)
        def _():
            copy.start()

    @pl.when(z + i <= last)
    def _():
        copy = chain_copy(buf, send, recv, z + i, 1, z - 1, remote)
        copy.wait_recv()

        @pl.when(z > 0)
        def _():
            copy.start()


def chain_end(buf, send, recv, z, last, remote):
    for origin in range(last + 1):
        @pl.when((z >= origin) & (z < last))
        def _():
            chain_copy(buf, send, recv, origin, 0, z + 1, remote).wait_send()

        @pl.when((z <= origin) & (z > 0))
        def _():
            chain_copy(buf, send, recv, origin, 1, z - 1, remote).wait_send()


def solution(mesh):
    n, n_tensor = mesh.shape["expert"], mesh.shape["tensor"]
    chips = n // 2
    grid_b = math.isqrt(chips)
    grid_a = chips // grid_b
    assert grid_a * grid_b == chips and chips == n_tensor

    def shards(picked_rows, w_gate, w_up, w_down, combine_gate, pick_owner, pick_row, residual_in, norm_gain, projection):
        _, cap, d_z = picked_rows.shape
        ff = w_gate.shape[2]
        tokens = residual_in.shape[0]
        k_dev = projection.shape[0]
        width = 384
        chunks = d_z // width
        seg = cap // n_tensor
        hbm = pl.BlockSpec(memory_space=pl.ANY)
        vmem = pl.BlockSpec(memory_space=pltpu.VMEM)
        dma = pltpu.SemaphoreType.DMA
        return pl.pallas_call(
            functools.partial(body, n, n_tensor, grid_a, grid_b, width),
            out_shape=jax.ShapeDtypeStruct((tokens, d_z), BF16),
            in_specs=[hbm, hbm, hbm, hbm, vmem, vmem, vmem, hbm, vmem, hbm],
            out_specs=vmem,
            scratch_shapes=[
                pltpu.VMEM((cap, d_z), BF16),
                pltpu.VMEM((d_z, ff), BF16),
                pltpu.VMEM((d_z, ff), BF16),
                pltpu.VMEM((ff, d_z), BF16),
                pltpu.VMEM((tokens, d_z), BF16),
                pltpu.VMEM((HALVES, cap, 2 * ff // HALVES), F32),
                pltpu.VMEM((HALVES, n_tensor, seg, 2 * ff // HALVES), BF16),
                pltpu.VMEM((HALVES, n_tensor, seg, 2 * ff // HALVES), BF16),
                pltpu.VMEM((HALVES, n_tensor, seg, ff // HALVES), BF16),
                pltpu.VMEM((chunks, chips, 2, cap, width), BF16),
                pltpu.VMEM((chunks, n_tensor, tokens, width), BF16),
                pltpu.VMEM((n * k_dev, d_z), BF16),
                pltpu.VMEM((chips, 2, tokens, cap), BF16),
                pltpu.VMEM((n_tensor, 8, tokens), F32),
                pltpu.VMEM((tokens, d_z), F32),
                dma((4 + 2 * HALVES,)),
                dma((2, HALVES, n_tensor)),
                dma((2, HALVES, n_tensor)),
                dma((HALVES, 2, n_tensor)),
                dma((HALVES, 2, n_tensor)),
                dma((chunks, chips, 2, 1)),
                dma((chunks, chips, 2)),
                dma((chunks, chips)),
                dma((chunks, chips)),
                dma((chunks, 2, n_tensor)),
                dma((chunks, 2, n_tensor)),
                dma((n_tensor,)),
                dma((n_tensor,)),
                dma((chips, 2)),
                dma((chips, 2)),
                dma((chips,)),
                dma((chips,)),
            ],
            compiler_params=pltpu.CompilerParams(
                collective_id=0, has_side_effects=True, vmem_limit_bytes=60 * 2**20
            ),
            name="layer",
        )(picked_rows, w_gate, w_up, w_down, combine_gate, pick_owner, pick_row, residual_in, norm_gain[None, :], projection)

    return jax.shard_map(
        shards,
        mesh=mesh,
        in_specs=(
            P("expert", None, "tensor"),
            P("expert", "tensor", None),
            P("expert", "tensor", None),
            P("expert", None, "tensor"),
            P("expert", None),
            P(),
            P(),
            P("expert", "tensor"),
            P("tensor"),
            P("expert", "tensor"),
        ),
        out_specs=P("expert", "tensor"),
        check_vma=False,
    )
```

time: 360 us -> 130 us (0.36)
  waiting for transfers between devices: 294 us -> 0 us
  Pallas kernels: 0 us -> 127 us
  matrix products: 28.8 us -> 0 us
  between operations: 13.2 us -> 0.01 us
  blocking collectives: 9.64 us -> 0 us
  other arithmetic: 7.22 us -> 0 us
  starting transfers between devices: 3.87 us -> 0 us
    all_gather x2 -> x0, waiting for transfers between devices: 146 us -> none  [the longest x1 99.5 us: shards(): lax.all_gather(projection, 'expert', axis=0, tiled=True)]
    pallas_call x0 -> x1, Pallas kernels: none -> 127 us  [shards(): pl.pallas_call(functools.partial(body, n, n_tensor, grid_a, grid_b, width...]
    psum x1 -> x0, waiting for transfers between devices: 119 us -> none  [shards(): gate_pre, up_pre = lax.psum((gate_part, up_part), 'tensor')]
    all_to_all x1 -> x0, waiting for transfers between devices: 29 us -> none  [shards(): lax.all_to_all(outgoing, 'expert', split_axis=0, concat_axis=0, tiled=True)]
    dot_general x5 -> x0, matrix products: 28.8 us -> none  [the longest x1 11.7 us: shards(): jnp.dot(full_normed, lax.all_gather(projection, 'expert', axis=0, tiled=T...]
    psum x1 -> x0, blocking collectives: 9.64 us -> none  [shards(): square_total = lax.psum(jnp.sum(mixed * mixed, axis=1), 'tensor')]
    another operation x2 -> x0, other arithmetic: 4.58 us -> none
    all_to_all x1 -> x0, starting transfers between devices: 3.79 us -> none  [shards(): lax.all_to_all(outgoing, 'expert', split_axis=0, concat_axis=0, tiled=True)]
  transfers between devices with their start and end apart: 4 -> 0, of which waited for: 4 -> 0; matrix products, arithmetic and copies ran while one was open for 1% -> 0% of each run, Pallas kernels for 0% -> 0%
where the time goes in v1:
time: 130 us
  Pallas kernels  127 us (98%)
  local copies, waits for them, and re-layouts  3.21 us (2%)
    pallas_call x1, Pallas kernels, shards(): pl.pallas_call(functools.partial(body, n, n_tensor, grid_a, grid_b, width...  127 us

profile of v1, /device:TPU:0, one launch (start us, length us, event | category | flops | bytes accessed | tf_op | source)
XLA Modules:
  0.0 129.8 jit_solution(13338096289828769641)
XLA Ops:
  0.0 1.3 broadcast_in_dim.3.gain_ref
  1.3 126.6 %layer.1 = bf16[192,1536]{1,0:T(8,128)(2,1)} custom-call(bf16[1,256,1536]{2,1,0:T(8,128)(2,1)} %rows_hbm.1, bf16[1,1536,1536]{2,1,0:T(8,128)(2,1)} %gate_hbm.1, bf16[1,1536,1536]{2,1,0:T(8,128)(2,1)} %up_hbm.1, bf16[1,1536,1536]{2,1,0:T(8,128)(2,1)} %down_hbm.1, f32[1,256]{1,0:T(1,128)} %combine_ref.1, s32[8,256]{1,0:T(8,128)} %owner_ref.1, ...), custom_call_target="tpu_custom_call" | custom-call | tf_op jit(solution)/shard_map/layer/pallas_call | solution.py:441
  127.9 1.9 %copy.12 = bf16[192,1536]{1,0:T(8,128)(2,1)} copy(bf16[192,1536]{1,0:T(8,128)(2,1)} %layer.1) | data formatting | bytes 1179648

commit v2 on v1

--- a/solution.py
+++ b/solution.py
@@ -13,6 +13,7 @@
 BF16 = jnp.bfloat16
 HI = lax.Precision.HIGHEST
 HALVES = 2
+PIECES = 3
 
 
 def body(
@@ -37,6 +38,7 @@
     tokens = resid.shape[0]
     k_dev = proj_hbm.shape[0]
     k_half = k_dev // 2
+    k_piece = k_half // PIECES
     offsets = [(da, db) for da in range(grid_a) for db in range(grid_b)]
 
     def chip_at(da, db):
@@ -84,17 +86,17 @@
     def slot(da, db):
         return da * grid_b + db
 
-    def proj_rows(da, db, k, half=None):
+    def proj_rows(da, db, k, half=None, piece=0):
         start = (chip_at(-da, -db) * 2 + k) * k_dev
         if half is None:
             return proj.at[pl.ds(pl.multiple_of(start, 16), k_dev)]
-        return proj.at[pl.ds(pl.multiple_of(start + half * k_half, 16), k_half)]
+        return proj.at[pl.ds(pl.multiple_of(start + half * k_half + piece * k_piece, 16), k_piece)]
 
     mine = proj.at[pl.ds(my_k, k_dev)]
     for da, db in offsets[1:]:
         if da == 0 or db == 0:
             begin(remote(proj_hbm, mine, p_send.at[slot(da, db), 0], p_recv.at[slot(da, db), 0], to_expert(da, db)))
-    begin(remote(proj_hbm, mine, p_sib_send.at[0], p_sib_recv.at[0], sibling))
+    begin(remote(proj_hbm, mine, p_sib_send.at[0, 0], p_sib_recv.at[0, 0], sibling))
 
     loads[0].wait()
     tile = 256
@@ -223,7 +225,7 @@
             s = slot(da, db)
             arrived(c_block(q, da, db, 1), c_sib_send.at[q, s], c_sib_recv.at[q, s])
             mixed += jnp.dot(table[s, 1], cbuf[q, s, 1], preferred_element_type=F32)
-        ebuf[q, z] = (mixed * gain_ref[:, cols]).astype(BF16)
+        ebuf[q, z] = (mixed * gain_ref[cols].reshape(1, width)).astype(BF16)
         chain_own(ebuf.at[q], e_send.at[q], e_recv.at[q], z, last, remote)
         return lax.dot_general(
             jnp.ones((8, width), F32), mixed * mixed, (((1,), (1,)), ((), ())), precision=HI,
@@ -236,11 +238,6 @@
             stage_send(t)
         if 0 <= t - 1 < chunks:
             stage_forward(t - 1)
-        if 0 <= t - 2 < chunks:
-            square_sum += stage_combine(t - 2)
-            for i in range(1, n_tensor):
-                if t - 2 - i >= 0:
-                    chain_pass(i, ebuf.at[t - 2 - i], e_send.at[t - 2 - i], e_recv.at[t - 2 - i], z, last, remote)
         if t == chunks:
             for da, db in offsets[1:]:
                 if da != 0 and db != 0:
@@ -251,14 +248,22 @@
                 if db == 0:
                     for d in range(1, grid_b):
                         u = slot(da, d)
-                        ref = proj_rows(da, 0, core, 0)
-                        begin(remote(ref, ref, p_send.at[u, 0], p_recv.at[u, 0], to_expert(0, d)))
+                        for piece in range(PIECES):
+                            ref = proj_rows(da, 0, core, 0, piece)
+                            begin(remote(ref, ref, p_send.at[u, piece], p_recv.at[u, piece], to_expert(0, d)))
                 else:
                     for d in range(1, grid_a):
                         u = slot(d, db)
-                        ref = proj_rows(0, db, core, 1)
-                        begin(remote(ref, ref, p_send.at[u, 1], p_recv.at[u, 1], to_expert(d, 0)))
-                begin(remote(block, block, p_sib_send.at[s], p_sib_recv.at[s], sibling))
+                        for piece in range(PIECES):
+                            ref = proj_rows(0, db, core, 1, piece)
+                            p = PIECES + piece
+                            begin(remote(ref, ref, p_send.at[u, p], p_recv.at[u, p], to_expert(d, 0)))
+                begin(remote(block, block, p_sib_send.at[s, 0], p_sib_recv.at[s, 0], sibling))
+        if 0 <= t - 2 < chunks:
+            square_sum += stage_combine(t - 2)
+            for i in range(1, n_tensor):
+                if t - 2 - i >= 0:
+                    chain_pass(i, ebuf.at[t - 2 - i], e_send.at[t - 2 - i], e_recv.at[t - 2 - i], z, last, remote)
 
     squares[z] = square_sum
     for i in range(1, n_tensor):
@@ -282,17 +287,29 @@
     inverse_rms = lax.rsqrt(column_total / (d_z * n_tensor) + 1e-05)
 
     loads[base + 2].wait()
-    order = [o for o in offsets if o[0] == 0 or o[1] == 0] + [o for o in offsets if o[0] != 0 and o[1] != 0]
-    for da, db in order:
-        if da != 0 and db != 0:
+    near = [o for o in offsets if o[0] == 0 or o[1] == 0]
+    far = [o for o in offsets if o[0] != 0 and o[1] != 0]
+    order = near + far
+
+    def hand_over(piece):
+        for da, db in far:
             s = slot(da, db)
             for half in range(2):
-                arrived(proj_rows(da, db, core, half), p_send.at[s, half], p_recv.at[s, half])
-            block = proj_rows(da, db, core)
-            begin(remote(block, block, p_sib_send.at[s], p_sib_recv.at[s], sibling))
+                p = half * PIECES + piece
+                block = proj_rows(da, db, core, half, piece)
+                arrived(block, p_send.at[s, p], p_recv.at[s, p])
+                begin(remote(block, block, p_sib_send.at[s, p], p_sib_recv.at[s, p], sibling))
+
+    assert len(near) >= PIECES
     for pos, (da, db) in enumerate(order):
         s = slot(da, db)
-        arrived(proj_rows(da, db, 1 - core), p_sib_send.at[s], p_sib_recv.at[s])
+        if pos < len(near):
+            arrived(proj_rows(da, db, 1 - core), p_sib_send.at[s, 0], p_sib_recv.at[s, 0])
+        else:
+            for half in range(2):
+                for piece in range(PIECES):
+                    p = half * PIECES + piece
+                    arrived(proj_rows(da, db, 1 - core, half, piece), p_sib_send.at[s, p], p_sib_recv.at[s, p])
         source = chip_at(-da, -db)
 
         @pl.loop(0, d_z // col)
@@ -306,6 +323,9 @@
                 out_ref[:, cols] = (total * inverse_rms).astype(BF16)
             else:
                 acc[:, cols] = total
+
+        if pos < PIECES:
+            hand_over(pos)
 
     for copy in sends:
         copy.wait_send()
@@ -472,16 +492,16 @@
                 dma((chunks, 2, n_tensor)),
                 dma((n_tensor,)),
                 dma((n_tensor,)),
-                dma((chips, 2)),
-                dma((chips, 2)),
-                dma((chips,)),
-                dma((chips,)),
+                dma((chips, 2 * PIECES)),
+                dma((chips, 2 * PIECES)),
+                dma((chips, 2 * PIECES)),
+                dma((chips, 2 * PIECES)),
             ],
             compiler_params=pltpu.CompilerParams(
                 collective_id=0, has_side_effects=True, vmem_limit_bytes=60 * 2**20
             ),
             name="layer",
-        )(picked_rows, w_gate, w_up, w_down, combine_gate, pick_owner, pick_row, residual_in, norm_gain[None, :], projection)
+        )(picked_rows, w_gate, w_up, w_down, combine_gate, pick_owner, pick_row, residual_in, norm_gain, projection)
 
     return jax.shard_map(
         shards,

time: 130 us -> 134 us (1.031)
  Pallas kernels: 127 us -> 132 us
    pallas_call x1, Pallas kernels: 127 us -> 132 us  [shards(): pl.pallas_call(functools.partial(body, n, n_tensor, grid_a, grid_b, width...]
where the time goes in v2:
time: 134 us
  Pallas kernels  132 us (99%)
  local copies, waits for them, and re-layouts  1.92 us (1%)
    pallas_call x1, Pallas kernels, shards(): pl.pallas_call(functools.partial(body, n, n_tensor, grid_a, grid_b, width...  132 us

profile of v2, /device:TPU:0, one launch (start us, length us, event | category | flops | bytes accessed | tf_op | source)
XLA Modules:
  0.0 133.8 jit_solution(10959181405238324474)
XLA Ops:
  0.0 131.9 %layer.1 = bf16[192,1536]{1,0:T(8,128)(2,1)} custom-call(bf16[1,256,1536]{2,1,0:T(8,128)(2,1)} %rows_hbm.1, bf16[1,1536,1536]{2,1,0:T(8,128)(2,1)} %gate_hbm.1, bf16[1,1536,1536]{2,1,0:T(8,128)(2,1)} %up_hbm.1, bf16[1,1536,1536]{2,1,0:T(8,128)(2,1)} %down_hbm.1, f32[1,256]{1,0:T(1,128)} %combine_ref.1, s32[8,256]{1,0:T(8,128)} %owner_ref.1, ...), custom_call_target="tpu_custom_call" | custom-call | tf_op jit(solution)/shard_map/layer/pallas_call | solution.py:461
  131.9 1.9 %copy.12 = bf16[192,1536]{1,0:T(8,128)(2,1)} copy(bf16[192,1536]{1,0:T(8,128)(2,1)} %layer.1) | data formatting | bytes 1179648

commit v3 on v2

--- a/solution.py
+++ b/solution.py
@@ -92,10 +92,30 @@
             return proj.at[pl.ds(pl.multiple_of(start, 16), k_dev)]
         return proj.at[pl.ds(pl.multiple_of(start + half * k_half + piece * k_piece, 16), k_piece)]
 
+    near = [o for o in offsets[1:] if o[0] == 0 or o[1] == 0]
+    far = [o for o in offsets if o[0] != 0 and o[1] != 0]
+
+    def near_span(da, late):
+        early = k_dev - k_piece
+        if da != 0:
+            return (early, k_piece) if late else (0, early)
+        return (0, k_piece) if late else (k_piece, early)
+
+    def near_rows(da, db, k, late):
+        start, size = near_span(da, late)
+        start += (chip_at(-da, -db) * 2 + k) * k_dev
+        return proj.at[pl.ds(pl.multiple_of(start, 16), size)]
+
+    def near_send(late):
+        for da, db in near:
+            start, size = near_span(da, late)
+            s = slot(da, db)
+            src = proj_hbm.at[pl.ds(start, size)]
+            dst = proj.at[pl.ds(pl.multiple_of(my_k + start, 16), size)]
+            begin(remote(src, dst, p_send.at[s, late], p_recv.at[s, late], to_expert(da, db)))
+
     mine = proj.at[pl.ds(my_k, k_dev)]
-    for da, db in offsets[1:]:
-        if da == 0 or db == 0:
-            begin(remote(proj_hbm, mine, p_send.at[slot(da, db), 0], p_recv.at[slot(da, db), 0], to_expert(da, db)))
+    near_send(0)
     begin(remote(proj_hbm, mine, p_sib_send.at[0, 0], p_sib_recv.at[0, 0], sibling))
 
     loads[0].wait()
@@ -238,13 +258,16 @@
             stage_send(t)
         if 0 <= t - 1 < chunks:
             stage_forward(t - 1)
+        if 0 <= t - 2 < chunks:
+            square_sum += stage_combine(t - 2)
+            for i in range(1, n_tensor):
+                if t - 2 - i >= 0:
+                    chain_pass(i, ebuf.at[t - 2 - i], e_send.at[t - 2 - i], e_recv.at[t - 2 - i], z, last, remote)
         if t == chunks:
-            for da, db in offsets[1:]:
-                if da != 0 and db != 0:
-                    continue
-                s = slot(da, db)
-                block = proj_rows(da, db, core)
-                arrived(block, p_send.at[s, 0], p_recv.at[s, 0])
+            near_send(1)
+            for da, db in near:
+                block = near_rows(da, db, core, 0)
+                arrived(block, p_send.at[slot(da, db), 0], p_recv.at[slot(da, db), 0])
                 if db == 0:
                     for d in range(1, grid_b):
                         u = slot(da, d)
@@ -258,12 +281,10 @@
                             ref = proj_rows(0, db, core, 1, piece)
                             p = PIECES + piece
                             begin(remote(ref, ref, p_send.at[u, p], p_recv.at[u, p], to_expert(d, 0)))
-                begin(remote(block, block, p_sib_send.at[s, 0], p_sib_recv.at[s, 0], sibling))
-        if 0 <= t - 2 < chunks:
-            square_sum += stage_combine(t - 2)
-            for i in range(1, n_tensor):
-                if t - 2 - i >= 0:
-                    chain_pass(i, ebuf.at[t - 2 - i], e_send.at[t - 2 - i], e_recv.at[t - 2 - i], z, last, remote)
+
+    for da, db in near:
+        block = near_rows(da, db, core, 0)
+        begin(remote(block, block, p_sib_send.at[slot(da, db), 0], p_sib_recv.at[slot(da, db), 0], sibling))
 
     squares[z] = square_sum
     for i in range(1, n_tensor):
@@ -287,9 +308,14 @@
     inverse_rms = lax.rsqrt(column_total / (d_z * n_tensor) + 1e-05)
 
     loads[base + 2].wait()
-    near = [o for o in offsets if o[0] == 0 or o[1] == 0]
-    far = [o for o in offsets if o[0] != 0 and o[1] != 0]
-    order = near + far
+    order = [(0, 0)] + near + far
+
+    def hand_over_late():
+        for da, db in near:
+            s = slot(da, db)
+            block = near_rows(da, db, core, 1)
+            arrived(block, p_send.at[s, 1], p_recv.at[s, 1])
+            begin(remote(block, block, p_sib_send.at[s, 1], p_sib_recv.at[s, 1], sibling))
 
     def hand_over(piece):
         for da, db in far:
@@ -300,11 +326,14 @@
                 arrived(block, p_send.at[s, p], p_recv.at[s, p])
                 begin(remote(block, block, p_sib_send.at[s, p], p_sib_recv.at[s, p], sibling))
 
-    assert len(near) >= PIECES
+    assert len(near) + 1 >= PIECES
     for pos, (da, db) in enumerate(order):
         s = slot(da, db)
-        if pos < len(near):
+        if pos == 0:
             arrived(proj_rows(da, db, 1 - core), p_sib_send.at[s, 0], p_sib_recv.at[s, 0])
+        elif pos <= len(near):
+            for late in range(2):
+                arrived(near_rows(da, db, 1 - core, late), p_sib_send.at[s, late], p_sib_recv.at[s, late])
         else:
             for half in range(2):
                 for piece in range(PIECES):
@@ -324,6 +353,8 @@
             else:
                 acc[:, cols] = total
 
+        if pos == 0:
+            hand_over_late()
         if pos < PIECES:
             hand_over(pos)
 

time: 134 us -> 124 us (0.925)
  Pallas kernels: 132 us -> 121 us
    pallas_call x1, Pallas kernels: 132 us -> 121 us  [shards(): pl.pallas_call(functools.partial(body, n, n_tensor, grid_a, grid_b, width...]
where the time goes in v3:
time: 124 us; the launch traced here: 123 us
  Pallas kernels  121 us (98%)
  local copies, waits for them, and re-layouts  1.92 us (2%)
    pallas_call x1, Pallas kernels, shards(): pl.pallas_call(functools.partial(body, n, n_tensor, grid_a, grid_b, width...  121 us

profile of v3, /device:TPU:0, one launch (start us, length us, event | category | flops | bytes accessed | tf_op | source)
XLA Modules:
  0.0 123.2 jit_solution(8881791421507839094)
XLA Ops:
  0.0 121.3 %layer.1 = bf16[192,1536]{1,0:T(8,128)(2,1)} custom-call(bf16[1,256,1536]{2,1,0:T(8,128)(2,1)} %rows_hbm.1, bf16[1,1536,1536]{2,1,0:T(8,128)(2,1)} %gate_hbm.1, bf16[1,1536,1536]{2,1,0:T(8,128)(2,1)} %up_hbm.1, bf16[1,1536,1536]{2,1,0:T(8,128)(2,1)} %down_hbm.1, f32[1,256]{1,0:T(1,128)} %combine_ref.1, s32[8,256]{1,0:T(8,128)} %owner_ref.1, ...), custom_call_target="tpu_custom_call" | custom-call | tf_op jit(solution)/shard_map/layer/pallas_call | solution.py:492
  121.3 1.9 %copy.12 = bf16[192,1536]{1,0:T(8,128)(2,1)} copy(bf16[192,1536]{1,0:T(8,128)(2,1)} %layer.1) | data formatting | bytes 1179648

commit v4 on v3

--- a/solution.py
+++ b/solution.py
@@ -12,7 +12,7 @@
 F32 = jnp.float32
 BF16 = jnp.bfloat16
 HI = lax.Precision.HIGHEST
-HALVES = 2
+HALVES = 3
 PIECES = 3
 
 

time: 124 us -> 129 us (1.040)
  Pallas kernels: 121 us -> 126 us
    pallas_call x1, Pallas kernels: 121 us -> 126 us  [shards(): pl.pallas_call(functools.partial(body, n, n_tensor, grid_a, grid_b, width...]
where the time goes in v4:
time: 129 us; the launch traced here: 128 us
  Pallas kernels  126 us (98%)
  local copies, waits for them, and re-layouts  1.92 us (1%)
    pallas_call x1, Pallas kernels, shards(): pl.pallas_call(functools.partial(body, n, n_tensor, grid_a, grid_b, width...  126 us

profile of v4, /device:TPU:0, one launch (start us, length us, event | category | flops | bytes accessed | tf_op | source)
XLA Modules:
  0.0 128.2 jit_solution(16768567844170041264)
XLA Ops:
  0.0 126.2 %layer.1 = bf16[192,1536]{1,0:T(8,128)(2,1)} custom-call(bf16[1,256,1536]{2,1,0:T(8,128)(2,1)} %rows_hbm.1, bf16[1,1536,1536]{2,1,0:T(8,128)(2,1)} %gate_hbm.1, bf16[1,1536,1536]{2,1,0:T(8,128)(2,1)} %up_hbm.1, bf16[1,1536,1536]{2,1,0:T(8,128)(2,1)} %down_hbm.1, f32[1,256]{1,0:T(1,128)} %combine_ref.1, s32[8,256]{1,0:T(8,128)} %owner_ref.1, ...), custom_call_target="tpu_custom_call" | custom-call | tf_op jit(solution)/shard_map/layer/pallas_call | solution.py:492
  126.2 1.9 %copy.12 = bf16[192,1536]{1,0:T(8,128)(2,1)} copy(bf16[192,1536]{1,0:T(8,128)(2,1)} %layer.1) | data formatting | bytes 1179648
